TPU v7x, 32 devices: a whole 2x2x4 slice. The times are simulated.
32 devices in a mesh: groups: 2 (over y), ctx: 16 (over z, x, core).
Axes of the slice: x: 2, y: 2, z: 4, core: 2. Of those that a mesh axis runs over, the one named last changes fastest.
Arguments:
- old_cache: bfloat16 [4096, 2048], P(('groups', 'ctx')), parts along dimension 0, may hold values from -10 to 10
- new_slot: int32 [4096], P(('groups', 'ctx')), parts along dimension 0, may hold values from -1 to 1023, as said below
- lengths: int32 [8], P('groups'), parts along dimension 0, may hold values from 1 to 768, 1024 in all
- old_angle: float32 [768, 64], replicated, may hold values from -3.15 to 3.15
- new_angle: float32 [768, 64], replicated, may hold values from -3.15 to 4.15
- queries: bfloat16 [64, 8192], P(('groups', 'ctx')), parts along dimension 0, may hold values from -128 to 128
- new_kv: bfloat16 [64, 2048], P(('groups', 'ctx')), parts along dimension 0, may hold values from -6 to 6
- resid: bfloat16 [64, 8192], P(('groups', 'ctx')), parts along dimension 0, may hold values from -6 to 6
- gain: bfloat16 [8192], replicated, may hold values from 0.25 to 1.75
- w_gate: bfloat16 [8192, 28672], P(None, 'ctx'), may hold values from -0.0625 to 0.0625
- w_up: bfloat16 [8192, 28672], P(None, 'ctx'), may hold values from -0.0625 to 0.0625
- w_down: bfloat16 [28672, 8192], P('ctx'), may hold values from -0.03125 to 0.03125
Outputs:
- new_cache: bfloat16 [2048, 2048], P(('groups', 'ctx')), parts along dimension 0
- layer_out: bfloat16 [64, 8192], P(('groups', 'ctx')), parts along dimension 0
There are 2 independent parts, one for each index of `groups`. A program takes and returns all parts, laid end to end along the dimension named above; an argument that names none is the same for every part. Nothing has to cross between parts.
Inputs may be any that keep to these rules, and one draw needn't show every extreme that they name: `new_slot`: for slots below 1024: distinct slots of the new layout; the tokens of each holding device go to every device of ctx, exactly 8 to each. Slots from 1024 on hold -1.
All inputs are finite; a program needn't handle non-finite values.
Results may differ from a plain program's by a relative error of at most 0.0057.
Values may be sent and summed in bfloat16 or wider, within the bound.
A program may use at most 128 MiB of HBM per device.

v0:
```python
import jax
import jax.numpy as jnp
from jax import lax
from jax.sharding import PartitionSpec as P

QH = 64
KVH = 8
HD = 128
CTOK_DEV = 64
SAMPLES = 4


def rotate_block(block, where_pos, old_angle, new_angle):
    rows_here = block.shape[0]
    half_size = HD // 2
    parts = block.reshape(rows_here, 2, KVH, HD)
    keys = parts[:, 0].astype(jnp.float32)
    delta = jnp.take(new_angle, where_pos, axis=0) - jnp.take(old_angle, where_pos, axis=0)
    cosine = jnp.cos(delta)[:, None, :]
    sine = jnp.sin(delta)[:, None, :]
    first = keys[..., :half_size]
    second = keys[..., half_size:]
    turned = jnp.concatenate(
        [first * cosine - second * sine, second * cosine + first * sine], axis=-1
    ).astype(jnp.bfloat16)
    return jnp.stack([turned, parts[:, 1]], axis=1).reshape(rows_here, 2 * KVH * HD)


def per_device(
    old_cache,
    new_slot,
    lengths,
    old_angle,
    new_angle,
    queries,
    new_kv,
    resid,
    gain,
    w_gate,
    w_up,
    w_down,
):
    devices = lax.axis_size("ctx")
    own_index = lax.axis_index("ctx")
    slot_count = old_cache.shape[0]
    row_width = old_cache.shape[1]
    per_peer = slot_count // devices
    rows_dev = queries.shape[0]
    all_rows = rows_dev * devices
    group_size = QH // KVH
    high = lax.Precision.HIGHEST
    scale = 1.0 / float(HD) ** 0.5
    tokens = own_index * slot_count + jnp.arange(slot_count, dtype=jnp.int32)
    row_ends = jnp.cumsum(lengths)
    passed = row_ends[None, :] <= tokens[:, None]
    owner_row = jnp.minimum(jnp.sum(passed.astype(jnp.int32), axis=1), lengths.shape[0] - 1)
    row_prior = jnp.sum(jnp.where(passed, lengths[None, :], 0), axis=1)
    position = jnp.clip(tokens - row_prior, 0, old_angle.shape[0] - 1)
    filled = new_slot >= 0
    all_queries = lax.all_gather(queries, "ctx", axis=0, tiled=True)
    target = jnp.where(
        filled, new_slot // CTOK_DEV, jnp.arange(slot_count, dtype=jnp.int32) // per_peer
    )
    sorted_order = jnp.argsort(target, stable=True)
    new_place = jnp.where(filled, new_slot % CTOK_DEV, -1)
    slot_info = jnp.stack([new_place, owner_row, position], axis=1)[sorted_order]
    sent_rows = old_cache[sorted_order].reshape(devices, per_peer, row_width)
    got_rows = lax.all_to_all(sent_rows, "ctx", split_axis=0, concat_axis=0, tiled=True)
    got_info = lax.all_to_all(
        slot_info.reshape(devices, per_peer, 3), "ctx", split_axis=0, concat_axis=0, tiled=True
    )
    got_rows = got_rows.reshape(slot_count, row_width)
    got_info = got_info.reshape(slot_count, 3)
    landing = jnp.where(got_info[:, 0] >= 0, got_info[:, 0], CTOK_DEV)
    placed = jnp.zeros((CTOK_DEV, row_width), jnp.bfloat16).at[landing].set(got_rows, mode="drop")
    placed_row = jnp.zeros((CTOK_DEV,), jnp.int32).at[landing].set(got_info[:, 1], mode="drop")
    placed_pos = jnp.zeros((CTOK_DEV,), jnp.int32).at[landing].set(got_info[:, 2], mode="drop")
    placed, moved_row, moved_pos = (placed, placed_row, placed_pos)
    new_cache = rotate_block(placed, moved_pos, old_angle, new_angle)
    key_count = new_cache.shape[0]
    key_split = new_cache.reshape(key_count, 2, KVH, HD)
    value_four = key_split[:, 1].astype(jnp.float32)
    query_four = all_queries.reshape(all_rows, KVH, group_size, HD)
    scores = (
        jnp.einsum(
            "mjge,cje->mjgc", query_four, key_split[:, 0], preferred_element_type=jnp.float32
        )
        * scale
    )
    query_row = jnp.arange(all_rows, dtype=jnp.int32) // (2 * SAMPLES)
    matching = query_row[:, None] == moved_row[None, :]
    scores = jnp.where(matching[:, None, None, :], scores, -1e30)
    local_top = jnp.max(scores, axis=-1)
    own_query = queries.reshape(rows_dev, KVH, group_size, HD).astype(jnp.float32)
    fresh_kv = jnp.repeat(new_kv.reshape(rows_dev // 2, 2, 2, KVH, HD), 2, axis=0).astype(
        jnp.float32
    )
    own_steps = (
        jnp.arange(2, dtype=jnp.int32)[None, :]
        <= (jnp.arange(rows_dev, dtype=jnp.int32) % 2)[:, None]
    )
    own_scores = jnp.einsum("mjge,msje->mjgs", own_query, fresh_kv[:, :, 0], precision=high) * scale
    own_scores = jnp.where(own_steps[:, None, None, :], own_scores, -1e30)
    own_top = jnp.max(own_scores, axis=-1)
    floor_top = jnp.maximum(local_top, -10000.0)
    weights_local = jnp.exp(scores - floor_top[..., None])
    summed = jnp.einsum("mjgc,cje->mjge", weights_local, value_four, precision=high)
    totals = jnp.sum(weights_local, axis=-1)
    got_sums, got_totals, got_tops = (
        lax.all_to_all(
            summed.reshape(devices, rows_dev, QH * HD),
            "ctx",
            split_axis=0,
            concat_axis=0,
            tiled=True,
        ),
        lax.all_to_all(
            totals.reshape(devices, rows_dev, QH), "ctx", split_axis=0, concat_axis=0, tiled=True
        ),
        lax.all_to_all(
            floor_top.reshape(devices, rows_dev, QH), "ctx", split_axis=0, concat_axis=0, tiled=True
        ),
    )
    got_tops = got_tops.reshape(devices, rows_dev, KVH, group_size)
    row_top = jnp.maximum(jnp.max(got_tops, axis=0), own_top)
    rescale = jnp.exp(got_tops - row_top[None])
    weights_own = jnp.exp(own_scores - row_top[..., None])
    row_sums = jnp.sum(
        rescale[..., None] * got_sums.reshape(devices, rows_dev, KVH, group_size, HD), axis=0
    )
    row_sums = row_sums + jnp.einsum(
        "mjgs,msje->mjge", weights_own, fresh_kv[:, :, 1], precision=high
    )
    row_totals = jnp.sum(
        rescale * got_totals.reshape(devices, rows_dev, KVH, group_size), axis=0
    ) + jnp.sum(weights_own, axis=-1)
    attn = (row_sums / row_totals[..., None]).reshape(rows_dev, QH * HD)
    hstate = resid.astype(jnp.float32) + attn
    normed = (
        hstate
        * lax.rsqrt(jnp.mean(hstate * hstate, axis=-1, keepdims=True) + 1e-05)
        * gain.astype(jnp.float32)
    ).astype(jnp.bfloat16)
    piece = lax.all_gather(normed, "ctx", axis=0, tiled=True)
    gate_out = jnp.dot(piece, w_gate, preferred_element_type=jnp.float32)
    up_out = jnp.dot(piece, w_up, preferred_element_type=jnp.float32)
    hidden_all = (jax.nn.silu(gate_out) * up_out).astype(jnp.bfloat16)
    ffn_out = lax.psum_scatter(
        jnp.dot(hidden_all, w_down, preferred_element_type=jnp.float32),
        "ctx",
        scatter_dimension=0,
        tiled=True,
    )
    layer_out = (hstate + ffn_out).astype(jnp.bfloat16)
    return (new_cache, layer_out)


def solution(mesh):
    return jax.shard_map(
        per_device,
        mesh=mesh,
        in_specs=(
            P(("groups", "ctx"), None),
            P(("groups", "ctx")),
            P("groups"),
            P(),
            P(),
            P(("groups", "ctx"), None),
            P(("groups", "ctx"), None),
            P(("groups", "ctx"), None),
            P(),
            P(None, "ctx"),
            P(None, "ctx"),
            P("ctx", None),
        ),
        out_specs=(P(("groups", "ctx"), None), P(("groups", "ctx"), None)),
        check_vma=False,
    )
```

profile of v0, /device:TPU:0, one launch (start us, length us, event | category | flops | bytes accessed | tf_op | source)
XLA Modules:
  0.0 276.3 jit_solution(13769297449490478126)
XLA Ops:
  7.2 0.9 reduce-window.8
  8.1 0.7 fusion.34
  8.9 0.7 compare_select_fusion.8
  9.5 2.5 sort.17
  12.2 0.6 gather_fusion
  12.8 0.8 copy.85
  13.6 7.4 %all-to-all-start = ((s32[16,8,3]{1,2,0:T(4,128)}), s32[16,8,3]{1,2,0:T(4,128)S(1)}, u32[]{:S(2)}, u32[]{:S(2)}) async-start(s32[16,8,3]{1,2,0:T(4,128)} %copy.85), calls=%async_computation | async-start | bytes 65536 | tf_op jit(solution)/shard_map/all_to_all | solution.py:69
  21.0 23.5 %all-gather = bf16[16,2,8192]{2,1,0:T(2,128)(2,1)S(1)} all-gather(bf16[1,2,8192]{2,1,0:T(2,128)(2,1)} %bitcast.116), channel_id=1, replica_groups=mesh['groups'=2,'ctx'=16] {'ctx'}, dimensions={0}, use_global_device_ids=true | all-gather | bytes 557056 | tf_op jit(solution)/shard_map/all_gather | solution.py:60
  44.4 1.1 copy.89
  45.5 1.1 copy.88
  46.6 1.7 gather_fusion.1
  48.4 0.4 reshape.274
  48.8 3.6 %all-to-all-start.1 = ((bf16[16,8,2048]{2,1,0:T(8,128)(2,1)}), bf16[16,8,2048]{2,1,0:T(8,128)(2,1)S(1)}, u32[]{:S(2)}, u32[]{:S(2)}) async-start(bf16[16,8,2048]{2,1,0:T(8,128)(2,1)} %bitcast.7), calls=%async_computation.1 | async-start | bytes 1048576 | tf_op jit(solution)/shard_map/all_to_all | solution.py:68
  52.5 1.0 scatter_custom_fusion.2
  53.5 1.0 scatter_custom_fusion.1
  54.5 0.6 gather_fusion.3
  55.1 0.6 gather_fusion.2
  56.0 10.8 %all-to-all-done.1 = bf16[16,8,2048]{2,1,0:T(8,128)(2,1)S(1)} async-done(((bf16[16,8,2048]{2,1,0:T(8,128)(2,1)}), bf16[16,8,2048]{2,1,0:T(8,128)(2,1)S(1)}, u32[]{:S(2)}, u32[]{:S(2)}) %all-to-all-start.1) | async-done | bytes 524320 | tf_op jit(solution)/shard_map/all_to_all | solution.py:68
  66.8 1.4 scatter_custom_fusion
  68.4 0.6 fusion.47
  69.3 0.7 reshape.368
  70.0 4.0 %all-to-all-start.2 = ((f32[16,1,128]{2,1,0:T(1,128)}), f32[16,1,128]{2,1,0:T(1,128)S(1)}, u32[]{:S(2)}, u32[]{:S(2)}) async-start(f32[16,1,128]{2,1,0:T(1,128)} %reshape.368), calls=%async_computation.2 | async-start | bytes 16384 | tf_op jit(solution)/shard_map/all_to_all | solution.py:120
  74.1 0.7 fusion.7
  74.9 0.7 reshape.370
  75.6 4.8 %all-to-all-done.2 = f32[16,1,128]{2,1,0:T(1,128)S(1)} async-done(((f32[16,1,128]{2,1,0:T(1,128)}), f32[16,1,128]{2,1,0:T(1,128)S(1)}, u32[]{:S(2)}, u32[]{:S(2)}) %all-to-all-start.2) | async-done | bytes 8224 | tf_op jit(solution)/shard_map/all_to_all | solution.py:120
  80.4 3.5 %all-to-all-start.4 = ((f32[16,1,128]{2,1,0:T(1,128)}), f32[16,1,128]{2,1,0:T(1,128)S(1)}, u32[]{:S(2)}, u32[]{:S(2)}) async-start(f32[16,1,128]{2,1,0:T(1,128)} %reshape.370), calls=%async_computation.4 | async-start | bytes 16384 | tf_op jit(solution)/shard_map/all_to_all | solution.py:117
  83.9 0.8 convolution_bitcast_fusion
  84.7 0.6 copy.97
  85.3 1.6 reshape.280
  86.9 3.3 %all-to-all-done.4 = f32[16,1,128]{2,1,0:T(1,128)S(1)} async-done(((f32[16,1,128]{2,1,0:T(1,128)}), f32[16,1,128]{2,1,0:T(1,128)S(1)}, u32[]{:S(2)}, u32[]{:S(2)}) %all-to-all-start.4) | async-done | bytes 8224 | tf_op jit(solution)/shard_map/all_to_all | solution.py:117
  90.2 3.7 %all-to-all-start.3 = ((f32[16,2,8192]{2,1,0:T(2,128)}), f32[16,2,8192]{2,1,0:T(2,128)S(1)}, u32[]{:S(2)}, u32[]{:S(2)}) async-start(f32[16,2,8192]{2,1,0:T(2,128)} %reshape.280), calls=%async_computation.3 | async-start | bytes 2097152 | tf_op jit(solution)/shard_map/all_to_all | solution.py:110
  93.9 0.7 copy.138
  94.7 0.9 fusion.48
  95.7 0.7 convert_element_type.39
  96.4 0.5 broadcast.231
  96.9 0.7 reduce.3
  98.1 0.7 reduce.4
  99.0 1.4 mul.99
  100.4 1.8 mul.100
  102.2 14.5 %all-to-all-done.3 = f32[16,2,8192]{2,1,0:T(2,128)S(1)} async-done(((f32[16,2,8192]{2,1,0:T(2,128)}), f32[16,2,8192]{2,1,0:T(2,128)S(1)}, u32[]{:S(2)}, u32[]{:S(2)}) %all-to-all-start.3) | async-done | bytes 1048608 | tf_op jit(solution)/shard_map/all_to_all | solution.py:110
  116.7 0.7 multiply_reduce_fusion
  118.0 24.3 %all-gather.1 = bf16[16,2,8192]{2,1,0:T(2,128)(2,1)S(1)} all-gather(bf16[1,2,8192]{2,1,0:T(2,128)(2,1)S(1)} %fusion.27), channel_id=1, replica_groups=mesh['groups'=2,'ctx'=16] {'ctx'}, dimensions={0}, use_global_device_ids=true | all-gather | bytes 557056 | tf_op jit(solution)/shard_map/all_gather | solution.py:144
  142.5 12.0 %fusion.49 = f32[32,1792]{1,0:T(8,128)S(1)} fusion(bf16[32,8192]{1,0:T(8,128)(2,1)S(1)} %reshape.349, bf16[8192,1792]{1,0:T(8,128)(2,1)} %param.23), kind=kOutput, calls=%fused_computation.115 | convolution fusion | flops 939524096 | bytes 30113792 | tf_op jit(solution)/shard_map/dot_general | solution.py:145
  154.4 22.6 %fusion.1 = f32[32,8192]{1,0:T(8,128)} fusion(bf16[1792,8192]{1,0:T(8,128)(2,1)} %param.25, bf16[32,8192]{1,0:T(8,128)(2,1)S(1)} %reshape.349, bf16[8192,1792]{1,0:T(8,128)(2,1)} %param.24, f32[32,1792]{1,0:T(8,128)S(1)} %fusion.49), kind=kOutput, calls=%fused_computation.9 | convolution fusion | flops 1879392256 | bytes 60522496 | tf_op jit(solution)/shard_map/dot_general | solution.py:149
  177.1 0.6 dynamic-slice
  178.7 0.8 copy.137
  179.5 88.4 %all-reduce.3.cloned.1.call-done = f32[32,8192]{1,0:T(8,128)} async-done(((f32[32,8192]{1,0:T(8,128)}), f32[32,8192]{1,0:T(8,128)}) %all-reduce.3.cloned.1.call-update) | async-done | bytes 1048592
  267.8 1.6 fusion.23
  (64 shorter events, 3.3 us)
Async XLA Ops:
  7.2 39.5 %copy-start = (bf16[128,2048]{1,0:T(8,128)(2,1)S(1)}, bf16[128,2048]{1,0:T(8,128)(2,1)}, u32[]{:S(2)}) copy-start(bf16[128,2048]{1,0:T(8,128)(2,1)} %param.14) | copy-start | bytes 1572868
  7.2 110.5 %copy-start.2 = (bf16[2,8192]{1,0:T(2,128)(2,1)S(1)}, bf16[2,8192]{1,0:T(2,128)(2,1)}, u32[]{:S(2)}) copy-start(bf16[2,8192]{1,0:T(2,128)(2,1)} %param.21) | copy-start | bytes 98308
  13.6 35.1 %all-to-all-start = ((s32[16,8,3]{1,2,0:T(4,128)}), s32[16,8,3]{1,2,0:T(4,128)S(1)}, u32[]{:S(2)}, u32[]{:S(2)}) async-start(s32[16,8,3]{1,2,0:T(4,128)} %copy.85), calls=%async_computation | async-start | bytes 65536 | tf_op jit(solution)/shard_map/all_to_all | solution.py:69
  48.8 18.0 %all-to-all-start.1 = ((bf16[16,8,2048]{2,1,0:T(8,128)(2,1)}), bf16[16,8,2048]{2,1,0:T(8,128)(2,1)S(1)}, u32[]{:S(2)}, u32[]{:S(2)}) async-start(bf16[16,8,2048]{2,1,0:T(8,128)(2,1)} %bitcast.7), calls=%async_computation.1 | async-start | bytes 1048576 | tf_op jit(solution)/shard_map/all_to_all | solution.py:68
  70.0 10.4 %all-to-all-start.2 = ((f32[16,1,128]{2,1,0:T(1,128)}), f32[16,1,128]{2,1,0:T(1,128)S(1)}, u32[]{:S(2)}, u32[]{:S(2)}) async-start(f32[16,1,128]{2,1,0:T(1,128)} %reshape.368), calls=%async_computation.2 | async-start | bytes 16384 | tf_op jit(solution)/shard_map/all_to_all | solution.py:120
  80.4 9.8 %all-to-all-start.4 = ((f32[16,1,128]{2,1,0:T(1,128)}), f32[16,1,128]{2,1,0:T(1,128)S(1)}, u32[]{:S(2)}, u32[]{:S(2)}) async-start(f32[16,1,128]{2,1,0:T(1,128)} %reshape.370), calls=%async_computation.4 | async-start | bytes 16384 | tf_op jit(solution)/shard_map/all_to_all | solution.py:117
  90.2 26.6 %all-to-all-start.3 = ((f32[16,2,8192]{2,1,0:T(2,128)}), f32[16,2,8192]{2,1,0:T(2,128)S(1)}, u32[]{:S(2)}, u32[]{:S(2)}) async-start(f32[16,2,8192]{2,1,0:T(2,128)} %reshape.280), calls=%async_computation.3 | async-start | bytes 2097152 | tf_op jit(solution)/shard_map/all_to_all | solution.py:110
  93.8 174.0 %all-reduce.3.cloned.1.call-start = ((), (), s32[]{:S(2)}) async-start(), calls=%async_computation.5 | async-start | bytes 2097152
  142.5 127.0 %copy-start.1 = (bf16[128,2048]{1,0:T(8,128)(2,1)S(1)}, bf16[128,2048]{1,0:T(8,128)(2,1)}, u32[]{:S(2)}) copy-start(bf16[128,2048]{1,0:T(8,128)(2,1)} %param.14) | copy-start | bytes 1572868
  154.4 22.7 %copy-start.3 = (u32[32]{0:T(128)S(1)}, u32[32]{0:T(128)}, u32[]{:S(2)}) copy-start(u32[32]{0:T(128)} %constant.120) | copy-start | bytes 388
Sparse Core Ops, SparseCore 0:
  177.2 90.5 all-reduce.2
where the time goes:
time: 277 us; the launch traced here: 276 us
  waiting for transfers between devices  122 us (44%)
  blocking collectives  47.7 us (17%)
  matrix products  37.2 us (13%)
  starting transfers between devices  22.1 us (8%)
  local copies, waits for them, and re-layouts  21.3 us (8%)
  between operations  15.1 us (5%)
  other arithmetic  11.1 us (4%)
    unnamed x2, waiting for transfers between devices  88.4 us
    all_gather x1, blocking collectives, per_device(): piece = lax.all_gather(normed, 'ctx', axis=0, tiled=True)  24.3 us
    all_gather x1, blocking collectives, per_device(): all_queries = lax.all_gather(queries, 'ctx', axis=0, tiled=True)  23.5 us
    dot_general x1, matrix products, per_device(): jnp.dot(hidden_all, w_down, preferred_element_type=jnp.float32)  22.6 us
    all_to_all x1, waiting for transfers between devices, per_device(): lax.all_to_all(summed.reshape(devices, rows_dev, QH * HD), 'ctx', split_a...  14.5 us
    dot_general x1, matrix products, per_device(): gate_out = jnp.dot(piece, w_gate, preferred_element_type=jnp.float32)  12 us
    all_to_all x1, waiting for transfers between devices, per_device(): lax.all_to_all(sent_rows, 'ctx', split_axis=0, concat_axis=0, tiled=True)  10.8 us
    all_to_all x1, starting transfers between devices, per_device(): lax.all_to_all(slot_info.reshape(devices, per_peer, 3), 'ctx', split_axis...  7.36 us
  transfers between devices with their start and end apart: 6, of which 5 were waited for; matrix products, arithmetic and copies ran while one was open for 8% of the time, Pallas kernels for 0%

commit v1 on v0

--- a/solution.py
+++ b/solution.py
@@ -51,7 +51,8 @@
     high = lax.Precision.HIGHEST
     scale = 1.0 / float(HD) ** 0.5
     tokens = own_index * slot_count + jnp.arange(slot_count, dtype=jnp.int32)
-    row_ends = jnp.cumsum(lengths)
+    requests = jnp.arange(lengths.shape[0], dtype=jnp.int32)
+    row_ends = jnp.sum(jnp.where(requests[None, :] <= requests[:, None], lengths[None, :], 0), axis=1)
     passed = row_ends[None, :] <= tokens[:, None]
     owner_row = jnp.minimum(jnp.sum(passed.astype(jnp.int32), axis=1), lengths.shape[0] - 1)
     row_prior = jnp.sum(jnp.where(passed, lengths[None, :], 0), axis=1)

time: 277 us -> 277 us (level)
  no operation moved by 1% of the time
where the time goes in v1:
time: 277 us; the launch traced here: 276 us
  waiting for transfers between devices  122 us (44%)
  blocking collectives  47.7 us (17%)
  matrix products  37.2 us (13%)
  starting transfers between devices  22.1 us (8%)
  local copies, waits for them, and re-layouts  21.3 us (8%)
  between operations  15.1 us (5%)
  other arithmetic  11 us (4%)
    unnamed x2, waiting for transfers between devices  88.4 us
    all_gather x1, blocking collectives, per_device(): piece = lax.all_gather(normed, 'ctx', axis=0, tiled=True)  24.3 us
    all_gather x1, blocking collectives, per_device(): all_queries = lax.all_gather(queries, 'ctx', axis=0, tiled=True)  23.5 us
    dot_general x1, matrix products, per_device(): jnp.dot(hidden_all, w_down, preferred_element_type=jnp.float32)  22.6 us
    all_to_all x1, waiting for transfers between devices, per_device(): lax.all_to_all(summed.reshape(devices, rows_dev, QH * HD), 'ctx', split_a...  14.5 us
    dot_general x1, matrix products, per_device(): gate_out = jnp.dot(piece, w_gate, preferred_element_type=jnp.float32)  12 us
    all_to_all x1, waiting for transfers between devices, per_device(): lax.all_to_all(sent_rows, 'ctx', split_axis=0, concat_axis=0, tiled=True)  10.8 us
    all_to_all x1, starting transfers between devices, per_device(): lax.all_to_all(slot_info.reshape(devices, per_peer, 3), 'ctx', split_axis...  7.35 us
  transfers between devices with their start and end apart: 6, of which 5 were waited for; matrix products, arithmetic and copies ran while one was open for 8% of the time, Pallas kernels for 0%

profile of v1, /device:TPU:0, one launch (start us, length us, event | category | flops | bytes accessed | tf_op | source)
XLA Modules:
  0.0 276.3 jit_solution(9601328087435192885)
XLA Ops:
  7.2 0.8 select_reduce_fusion
  8.0 0.7 fusion.34
  8.8 0.7 compare_select_fusion.8
  9.5 2.5 sort.17
  12.1 0.6 gather_fusion
  12.8 0.8 copy.85
  13.6 7.4 %all-to-all-start = ((s32[16,8,3]{1,2,0:T(4,128)}), s32[16,8,3]{1,2,0:T(4,128)S(1)}, u32[]{:S(2)}, u32[]{:S(2)}) async-start(s32[16,8,3]{1,2,0:T(4,128)} %copy.85), calls=%async_computation | async-start | bytes 65536 | tf_op jit(solution)/shard_map/all_to_all | solution.py:70
  20.9 23.5 %all-gather = bf16[16,2,8192]{2,1,0:T(2,128)(2,1)S(1)} all-gather(bf16[1,2,8192]{2,1,0:T(2,128)(2,1)} %bitcast.114), channel_id=1, replica_groups=mesh['groups'=2,'ctx'=16] {'ctx'}, dimensions={0}, use_global_device_ids=true | all-gather | bytes 557056 | tf_op jit(solution)/shard_map/all_gather | solution.py:61
  44.4 1.1 copy.89
  45.5 1.1 copy.88
  46.6 1.7 gather_fusion.1
  48.3 0.4 reshape.249
  48.7 3.6 %all-to-all-start.1 = ((bf16[16,8,2048]{2,1,0:T(8,128)(2,1)}), bf16[16,8,2048]{2,1,0:T(8,128)(2,1)S(1)}, u32[]{:S(2)}, u32[]{:S(2)}) async-start(bf16[16,8,2048]{2,1,0:T(8,128)(2,1)} %bitcast.5), calls=%async_computation.1 | async-start | bytes 1048576 | tf_op jit(solution)/shard_map/all_to_all | solution.py:69
  52.4 1.0 scatter_custom_fusion.2
  53.4 1.0 scatter_custom_fusion.1
  54.4 0.6 gather_fusion.3
  55.0 0.6 gather_fusion.2
  55.9 10.8 %all-to-all-done.1 = bf16[16,8,2048]{2,1,0:T(8,128)(2,1)S(1)} async-done(((bf16[16,8,2048]{2,1,0:T(8,128)(2,1)}), bf16[16,8,2048]{2,1,0:T(8,128)(2,1)S(1)}, u32[]{:S(2)}, u32[]{:S(2)}) %all-to-all-start.1) | async-done | bytes 524320 | tf_op jit(solution)/shard_map/all_to_all | solution.py:69
  66.7 1.4 scatter_custom_fusion
  68.4 0.6 fusion.47
  69.3 0.7 reshape.343
  70.0 4.0 %all-to-all-start.2 = ((f32[16,1,128]{2,1,0:T(1,128)}), f32[16,1,128]{2,1,0:T(1,128)S(1)}, u32[]{:S(2)}, u32[]{:S(2)}) async-start(f32[16,1,128]{2,1,0:T(1,128)} %reshape.343), calls=%async_computation.2 | async-start | bytes 16384 | tf_op jit(solution)/shard_map/all_to_all | solution.py:121
  74.0 0.7 fusion.7
  74.9 0.7 reshape.345
  75.6 4.8 %all-to-all-done.2 = f32[16,1,128]{2,1,0:T(1,128)S(1)} async-done(((f32[16,1,128]{2,1,0:T(1,128)}), f32[16,1,128]{2,1,0:T(1,128)S(1)}, u32[]{:S(2)}, u32[]{:S(2)}) %all-to-all-start.2) | async-done | bytes 8224 | tf_op jit(solution)/shard_map/all_to_all | solution.py:121
  80.3 3.5 %all-to-all-start.4 = ((f32[16,1,128]{2,1,0:T(1,128)}), f32[16,1,128]{2,1,0:T(1,128)S(1)}, u32[]{:S(2)}, u32[]{:S(2)}) async-start(f32[16,1,128]{2,1,0:T(1,128)} %reshape.345), calls=%async_computation.4 | async-start | bytes 16384 | tf_op jit(solution)/shard_map/all_to_all | solution.py:118
  83.8 0.8 convolution_bitcast_fusion
  84.6 0.6 copy.97
  85.2 1.6 reshape.255
  86.8 3.3 %all-to-all-done.4 = f32[16,1,128]{2,1,0:T(1,128)S(1)} async-done(((f32[16,1,128]{2,1,0:T(1,128)}), f32[16,1,128]{2,1,0:T(1,128)S(1)}, u32[]{:S(2)}, u32[]{:S(2)}) %all-to-all-start.4) | async-done | bytes 8224 | tf_op jit(solution)/shard_map/all_to_all | solution.py:118
  90.1 3.7 %all-to-all-start.3 = ((f32[16,2,8192]{2,1,0:T(2,128)}), f32[16,2,8192]{2,1,0:T(2,128)S(1)}, u32[]{:S(2)}, u32[]{:S(2)}) async-start(f32[16,2,8192]{2,1,0:T(2,128)} %reshape.255), calls=%async_computation.3 | async-start | bytes 2097152 | tf_op jit(solution)/shard_map/all_to_all | solution.py:111
  93.8 0.7 copy.138
  94.6 0.9 fusion.48
  95.6 0.7 convert_element_type.39
  96.3 0.5 broadcast.232
  96.9 0.7 reduce.3
  98.0 0.7 reduce.4
  98.9 1.4 mul.99
  100.3 1.8 mul.100
  102.2 14.5 %all-to-all-done.3 = f32[16,2,8192]{2,1,0:T(2,128)S(1)} async-done(((f32[16,2,8192]{2,1,0:T(2,128)}), f32[16,2,8192]{2,1,0:T(2,128)S(1)}, u32[]{:S(2)}, u32[]{:S(2)}) %all-to-all-start.3) | async-done | bytes 1048608 | tf_op jit(solution)/shard_map/all_to_all | solution.py:111
  116.7 0.7 multiply_reduce_fusion
  117.9 24.3 %all-gather.1 = bf16[16,2,8192]{2,1,0:T(2,128)(2,1)S(1)} all-gather(bf16[1,2,8192]{2,1,0:T(2,128)(2,1)S(1)} %fusion.27), channel_id=1, replica_groups=mesh['groups'=2,'ctx'=16] {'ctx'}, dimensions={0}, use_global_device_ids=true | all-gather | bytes 557056 | tf_op jit(solution)/shard_map/all_gather | solution.py:145
  142.4 12.0 %fusion.49 = f32[32,1792]{1,0:T(8,128)S(1)} fusion(bf16[32,8192]{1,0:T(8,128)(2,1)S(1)} %reshape.324, bf16[8192,1792]{1,0:T(8,128)(2,1)} %param.23), kind=kOutput, calls=%fused_computation.117 | convolution fusion | flops 939524096 | bytes 30113792 | tf_op jit(solution)/shard_map/dot_general | solution.py:146
  154.4 22.6 %fusion.1 = f32[32,8192]{1,0:T(8,128)} fusion(bf16[1792,8192]{1,0:T(8,128)(2,1)} %param.25, bf16[32,8192]{1,0:T(8,128)(2,1)S(1)} %reshape.324, bf16[8192,1792]{1,0:T(8,128)(2,1)} %param.24, f32[32,1792]{1,0:T(8,128)S(1)} %fusion.49), kind=kOutput, calls=%fused_computation.9 | convolution fusion | flops 1879392256 | bytes 60522496 | tf_op jit(solution)/shard_map/dot_general | solution.py:150
  177.1 0.6 dynamic-slice
  178.6 0.8 copy.137
  179.4 88.4 %all-reduce.3.cloned.1.call-done = f32[32,8192]{1,0:T(8,128)} async-done(((f32[32,8192]{1,0:T(8,128)}), f32[32,8192]{1,0:T(8,128)}) %all-reduce.3.cloned.1.call-update) | async-done | bytes 1048592
  267.8 1.6 fusion.23
  (64 shorter events, 3.3 us)
Async XLA Ops:
  7.2 39.4 %copy-start = (bf16[128,2048]{1,0:T(8,128)(2,1)S(1)}, bf16[128,2048]{1,0:T(8,128)(2,1)}, u32[]{:S(2)}) copy-start(bf16[128,2048]{1,0:T(8,128)(2,1)} %param.14) | copy-start | bytes 1572868
  7.2 110.4 %copy-start.2 = (bf16[2,8192]{1,0:T(2,128)(2,1)S(1)}, bf16[2,8192]{1,0:T(2,128)(2,1)}, u32[]{:S(2)}) copy-start(bf16[2,8192]{1,0:T(2,128)(2,1)} %param.21) | copy-start | bytes 98308
  13.6 35.1 %all-to-all-start = ((s32[16,8,3]{1,2,0:T(4,128)}), s32[16,8,3]{1,2,0:T(4,128)S(1)}, u32[]{:S(2)}, u32[]{:S(2)}) async-start(s32[16,8,3]{1,2,0:T(4,128)} %copy.85), calls=%async_computation | async-start | bytes 65536 | tf_op jit(solution)/shard_map/all_to_all | solution.py:70
  48.7 18.0 %all-to-all-start.1 = ((bf16[16,8,2048]{2,1,0:T(8,128)(2,1)}), bf16[16,8,2048]{2,1,0:T(8,128)(2,1)S(1)}, u32[]{:S(2)}, u32[]{:S(2)}) async-start(bf16[16,8,2048]{2,1,0:T(8,128)(2,1)} %bitcast.5), calls=%async_computation.1 | async-start | bytes 1048576 | tf_op jit(solution)/shard_map/all_to_all | solution.py:69
  70.0 10.4 %all-to-all-start.2 = ((f32[16,1,128]{2,1,0:T(1,128)}), f32[16,1,128]{2,1,0:T(1,128)S(1)}, u32[]{:S(2)}, u32[]{:S(2)}) async-start(f32[16,1,128]{2,1,0:T(1,128)} %reshape.343), calls=%async_computation.2 | async-start | bytes 16384 | tf_op jit(solution)/shard_map/all_to_all | solution.py:121
  80.3 9.8 %all-to-all-start.4 = ((f32[16,1,128]{2,1,0:T(1,128)}), f32[16,1,128]{2,1,0:T(1,128)S(1)}, u32[]{:S(2)}, u32[]{:S(2)}) async-start(f32[16,1,128]{2,1,0:T(1,128)} %reshape.345), calls=%async_computation.4 | async-start | bytes 16384 | tf_op jit(solution)/shard_map/all_to_all | solution.py:118
  90.1 26.6 %all-to-all-start.3 = ((f32[16,2,8192]{2,1,0:T(2,128)}), f32[16,2,8192]{2,1,0:T(2,128)S(1)}, u32[]{:S(2)}, u32[]{:S(2)}) async-start(f32[16,2,8192]{2,1,0:T(2,128)} %reshape.255), calls=%async_computation.3 | async-start | bytes 2097152 | tf_op jit(solution)/shard_map/all_to_all | solution.py:111
  93.8 174.0 %all-reduce.3.cloned.1.call-start = ((), (), s32[]{:S(2)}) async-start(), calls=%async_computation.5 | async-start | bytes 2097152
  142.4 127.0 %copy-start.1 = (bf16[128,2048]{1,0:T(8,128)(2,1)S(1)}, bf16[128,2048]{1,0:T(8,128)(2,1)}, u32[]{:S(2)}) copy-start(bf16[128,2048]{1,0:T(8,128)(2,1)} %param.14) | copy-start | bytes 1572868
  154.4 22.7 %copy-start.3 = (u32[32]{0:T(128)S(1)}, u32[32]{0:T(128)}, u32[]{:S(2)}) copy-start(u32[32]{0:T(128)} %constant.117) | copy-start | bytes 388
Sparse Core Ops, SparseCore 0:
  177.2 90.5 all-reduce.2

commit v2 on v1

--- a/solution.py
+++ b/solution.py
@@ -1,6 +1,8 @@
 import jax
 import jax.numpy as jnp
 from jax import lax
+from jax.experimental import pallas as pl
+from jax.experimental.pallas import tpu as pltpu
 from jax.sharding import PartitionSpec as P
 
 QH = 64
@@ -8,6 +10,427 @@
 HD = 128
 CTOK_DEV = 64
 SAMPLES = 4
+
+N = 16
+HOLD = 8
+PEER = 8
+GROUP = QH // KVH
+ROWS = 16
+KC = 512
+NG = 10
+DC = 1024
+ND = 3
+MESH = pl.DeviceIdType.MESH
+
+
+def remote(src, dst, send_sem, recv_sem, dev):
+    return pltpu.make_async_remote_copy(
+        src_ref=src,
+        dst_ref=dst,
+        send_sem=send_sem,
+        recv_sem=recv_sem,
+        device_id={"ctx": dev},
+        device_id_type=MESH,
+    )
+
+
+def dot(a, b, dims=((1,), (0,))):
+    return lax.dot_general(a, b, (dims, ((), ())), preferred_element_type=jnp.float32)
+
+
+def split_dot(a, b):
+    hi = a.astype(jnp.bfloat16)
+    lo = (a - hi.astype(jnp.float32)).astype(jnp.bfloat16)
+    return dot(hi, b) + dot(lo, b)
+
+
+def kernel(
+    old_cache, slots, lengths, old_angle, new_angle, pack, resid, gain,
+    w_gate, w_up, w_down,
+    new_cache, out,
+    wg, wu, wd, kv, kvr, packr, sent, got, attn, attnr, norm, wide, xs, accg, accu,
+    hidden, obuf, sbuf, rbuf, hst,
+    g_sem, u_sem, d_sem, kv_s, kv_r, p_s, p_r, a_s, a_r, n_s, n_r, t_s, t_r, f_s, f_r,
+):
+    f32, bf16 = jnp.float32, jnp.bfloat16
+    me = lax.axis_index("ctx")
+    steps = w_gate.shape[0] // KC
+    dsteps = w_down.shape[1] // DC
+    holds = me < HOLD
+
+    def fetch_in(c, s):
+        rows = pl.ds(pl.multiple_of(c * KC, KC), KC)
+        return (
+            pltpu.make_async_copy(w_gate.at[rows, :], wg.at[s], g_sem.at[s]),
+            pltpu.make_async_copy(w_up.at[rows, :], wu.at[s], u_sem.at[s]),
+        )
+
+    def fetch_out(c, s):
+        cols = pl.ds(pl.multiple_of(c * DC, DC), DC)
+        return pltpu.make_async_copy(w_down.at[:, cols], wd.at[s], d_sem.at[s])
+
+    barrier = pltpu.get_barrier_semaphore()
+
+    @pl.loop(1, N)
+    def _(k):
+        pl.semaphore_signal(
+            barrier, inc=1, device_id={"ctx": lax.rem(me + k, N)}, device_id_type=MESH
+        )
+
+    @pl.loop(0, NG)
+    def _(c):
+        a, b = fetch_in(c, c)
+        a.start()
+        b.start()
+
+    @pl.loop(0, ND)
+    def _(c):
+        fetch_out(c, c).start()
+
+    ends = [lengths[0]]
+    for i in range(1, 4):
+        ends.append(ends[-1] + lengths[i])
+
+    @pl.when(holds)
+    def _():
+        tok = me * 128 + lax.broadcasted_iota(jnp.int32, (128, 1), 0)
+        prior = jnp.zeros((128, 1), jnp.int32)
+        for i in range(4):
+            prior = prior + jnp.where(tok >= ends[i], lengths[i], 0)
+        places = old_angle.shape[0]
+        pos = jnp.clip(tok - prior, 0, places - 1)
+        pick = (lax.broadcasted_iota(jnp.int32, (128, places), 1) == pos).astype(f32).astype(bf16)
+        d = new_angle[...] - old_angle[...]
+        d1 = d.astype(bf16)
+        rest = d - d1.astype(f32)
+        d2 = rest.astype(bf16)
+        d3 = (rest - d2.astype(f32)).astype(bf16)
+        delta = dot(pick, d1) + dot(pick, d2) + dot(pick, d3)
+        delta = jnp.concatenate([delta, delta], axis=1)
+        lane = lax.broadcasted_iota(jnp.int32, (128, 128), 1)
+        cosine = jnp.cos(delta)
+        sine = jnp.sin(delta)
+        sine = jnp.where(lane < HD // 2, -sine, sine)
+        for j in range(KVH):
+            k = old_cache[:, j * HD:(j + 1) * HD].astype(f32)
+            kv[j, 0] = (k * cosine + pltpu.roll(k, HD // 2, 1) * sine).astype(bf16)
+            kv[j, 1] = old_cache[:, (KVH + j) * HD:(KVH + j + 1) * HD]
+
+    pl.semaphore_wait(barrier, N - 1)
+
+    @pl.loop(1, N)
+    def _(k):
+        to = lax.rem(me + k, N)
+
+        @pl.when(to < HOLD)
+        def _():
+            remote(pack.at[to], packr.at[me], p_s.at[to], p_r.at[me], to).start()
+
+    @pl.when(holds)
+    def _():
+        @pl.loop(1, HOLD)
+        def _(k):
+            to = lax.rem(me + k, HOLD)
+            remote(kv.at[to], kvr.at[me], kv_s.at[to], kv_r.at[me], to).start()
+
+        packr[me] = pack[me]
+        kvr[me] = kv[me]
+
+        slot_l = slots[...]
+        row_i = lax.broadcasted_iota(jnp.int32, (128, 128), 0)
+        col_i = lax.broadcasted_iota(jnp.int32, (128, 128), 1)
+        target_l = jnp.broadcast_to(lax.shift_right_arithmetic(slot_l, 6), (128, 128))
+        target_s = jnp.sum(
+            jnp.where(row_i == col_i, target_l, 0).astype(f32), axis=1, keepdims=True
+        ).astype(jnp.int32)
+        ahead = (target_s == target_l) & (row_i < col_i)
+        rank = jnp.sum(ahead.astype(f32), axis=0, keepdims=True).astype(jnp.int32)
+        dest = target_l * PEER + rank
+        perm = (row_i == dest).astype(f32)
+        place = jnp.sum(
+            perm * jnp.bitwise_and(slot_l, CTOK_DEV - 1).astype(f32), axis=1, keepdims=True
+        )
+        perm = perm.astype(bf16)
+        place = jnp.broadcast_to(place, (128, 128)).reshape(N, PEER, 128)
+        sent[:, :, KVH * HD:] = jnp.concatenate([place, place], axis=1).astype(bf16)
+        for j in range(KVH):
+            ks = dot(perm, kv[j, 0]).reshape(N, PEER, HD)
+            vs = dot(perm, kv[j, 1]).reshape(N, PEER, HD)
+            sent[:, :, j * HD:(j + 1) * HD] = jnp.concatenate([ks, vs], axis=1).astype(bf16)
+
+        @pl.loop(1, N)
+        def _(k):
+            frm = lax.rem(me + k, N)
+            remote(pack.at[0], packr.at[frm], p_s.at[0], p_r.at[frm], frm).wait_recv()
+
+        @pl.loop(1, HOLD)
+        def _(k):
+            frm = lax.rem(me + k, HOLD)
+            remote(kv.at[0], kvr.at[frm], kv_s.at[0], kv_r.at[frm], frm).wait_recv()
+
+        scale = 1.0 / float(HD) ** 0.5
+        q = packr[:, 0:16].reshape(256, HD)
+        k_own = packr[:, 16:32].reshape(256, HD)
+        v_own = packr[:, 32:48].reshape(256, HD)
+        k_all = kvr[:, 0].reshape(HOLD * 128, HD)
+        v_all = kvr[:, 1].reshape(HOLD * 128, HD)
+        s1 = dot(q, k_all, ((1,), (1,))) * scale
+        s2 = dot(q, k_own, ((1,), (1,))) * scale
+        tok = lax.broadcasted_iota(jnp.int32, (1, HOLD * 128), 1)
+        row_of = jnp.zeros((1, HOLD * 128), jnp.int32)
+        for i in range(4):
+            row_of = row_of + (tok >= ends[i]).astype(jnp.int32)
+        request = lax.broadcasted_iota(jnp.int32, (256, 1), 0) // 64
+        s1 = jnp.where(request == row_of, s1, -1e30)
+        qi = lax.broadcasted_iota(jnp.int32, (256, 256), 0)
+        ni = lax.broadcasted_iota(jnp.int32, (256, 256), 1)
+        mine = (qi // 16 == ni // 16) & (ni % 16 <= (qi % 16) // 8)
+        s2 = jnp.where(mine, s2, -1e30)
+        top = jnp.maximum(
+            jnp.max(s1, axis=1, keepdims=True), jnp.max(s2, axis=1, keepdims=True)
+        )
+        w1 = jnp.exp(s1 - top)
+        w2 = jnp.exp(s2 - top)
+        total = jnp.sum(w1, axis=1, keepdims=True) + jnp.sum(w2, axis=1, keepdims=True)
+        res = (split_dot(w1, v_all) + split_dot(w2, v_own)) / total
+        attn[...] = res.reshape(N, ROWS, HD)
+        attnr[me] = attn[me]
+
+        @pl.loop(1, N)
+        def _(k):
+            to = lax.rem(me + k, N)
+            remote(attn.at[to], attnr.at[me], a_s.at[to], a_r.at[me], to).start()
+
+    @pl.loop(0, HOLD)
+    def _(frm):
+        @pl.when(frm != me)
+        def _():
+            other = lax.rem(me + 1, N)
+            remote(attn.at[0], attnr.at[frm], a_s.at[0], a_r.at[frm], other).wait_recv()
+
+    h = resid[...].astype(f32) + attnr[...]
+    hst[...] = h
+    h4 = h.reshape(KVH, 2, GROUP, HD)
+    sq = jnp.sum(jnp.sum(h4 * h4, axis=0), axis=-1, keepdims=True)
+    mean = jnp.sum(sq, axis=1, keepdims=True) / float(KVH * GROUP * HD)
+    inv = lax.rsqrt(mean + 1e-05)
+    normed = h4 * inv[None] * gain[...].astype(f32).reshape(KVH, 1, GROUP, HD)
+    norm[me] = normed.reshape(KVH, ROWS, HD).astype(bf16)
+
+    z, x, core = me // 4, lax.rem(me // 2, 2), lax.rem(me, 2)
+
+    def at(zz, xx, cc):
+        return zz * 4 + xx * 2 + cc
+
+    x_peer, c_peer = at(z, 1 - x, core), at(z, x, 1 - core)
+
+    def push(block, sem, to):
+        return remote(norm.at[block], norm.at[block], n_s.at[sem], n_r.at[block], to)
+
+    for i in range(1, 4):
+        push(me, i - 1, at(lax.rem(z + i, 4), x, core)).start()
+    push(me, 3, x_peer).start()
+    push(me, 4, c_peer).start()
+    for i in range(1, 4):
+        block = at(lax.rem(z + i, 4), x, core)
+        push(block, 0, x_peer).wait_recv()
+        push(block, 3 + 2 * i, x_peer).start()
+        push(block, 4 + 2 * i, c_peer).start()
+    for i in range(4):
+        block = at(lax.rem(z + i, 4), 1 - x, core)
+        push(block, 0, x_peer).wait_recv()
+        push(block, 11 + i, c_peer).start()
+
+    @pl.loop(0, N // 2)
+    def _(i):
+        push(i * 2 + 1 - core, 0, x_peer).wait_recv()
+
+    @pl.when(holds)
+    def _():
+        @pl.loop(1, N)
+        def _(k):
+            to = lax.rem(me + k, N)
+            remote(sent.at[to], got.at[me], t_s.at[to], t_r.at[me], to).start()
+
+        got[me] = sent[me]
+
+    for j in range(KVH):
+        wide[...] = norm[:, j].reshape(256, HD).astype(f32)
+        for g in range(GROUP):
+            part = wide[pl.ds(g, 32, stride=GROUP), :].astype(bf16)
+            xs[2 * j + g // 4, :, (g % 4) * HD:(g % 4 + 1) * HD] = part
+
+    accg[...] = jnp.zeros_like(accg)
+    accu[...] = jnp.zeros_like(accu)
+
+    @pl.loop(0, steps)
+    def _(c):
+        s = lax.rem(c, NG)
+        a, b = fetch_in(c, s)
+        a.wait()
+        accg[...] += dot(xs[c], wg[s])
+        b.wait()
+        accu[...] += dot(xs[c], wu[s])
+
+        @pl.when(c + NG < steps)
+        def _():
+            a2, b2 = fetch_in(c + NG, s)
+            a2.start()
+            b2.start()
+
+    gate = accg[...]
+    hidden[...] = (gate / (1.0 + jnp.exp(-gate)) * accu[...]).astype(bf16)
+
+    def give(c, to):
+        return remote(
+            sbuf.at[c, to], rbuf.at[c, me], f_s.at[c, to], f_r.at[c, me], to
+        )
+
+    @pl.loop(0, dsteps)
+    def _(c):
+        s = lax.rem(c, ND)
+        fetch_out(c, s).wait()
+        part = dot(hidden[...], wd[s])
+        for g in range(GROUP):
+            obuf[pl.ds(g, 32, stride=GROUP), :] = part[:, g * HD:(g + 1) * HD]
+        sbuf[c] = obuf[...].reshape(N, ROWS, HD).astype(bf16)
+
+        @pl.when(c + ND < dsteps)
+        def _():
+            fetch_out(c + ND, s).start()
+
+        rbuf[c, me] = sbuf[c, me]
+
+        @pl.loop(1, N)
+        def _(k):
+            give(c, lax.rem(me + k, N)).start()
+
+    @pl.loop(0, HOLD)
+    def _(frm):
+        @pl.when(frm != me)
+        def _():
+            other = lax.rem(me + 1, N)
+            remote(sent.at[0], got.at[frm], t_s.at[0], t_r.at[frm], other).wait_recv()
+
+    rows = HOLD * PEER
+    where = got[:, :, KVH * HD:].astype(f32)[:, 0:PEER].reshape(rows, 128)
+    lane = lax.broadcasted_iota(jnp.int32, (rows, 128), 1).astype(f32)
+    put = (where == lane).astype(f32).astype(bf16)
+    for j in range(KVH):
+        both = got[:, :, j * HD:(j + 1) * HD].astype(f32)
+        ks = both[:, 0:PEER].reshape(rows, HD).astype(bf16)
+        vs = both[:, PEER:].reshape(rows, HD).astype(bf16)
+        new_k = dot(put, ks, ((0,), (0,)))[0:CTOK_DEV]
+        new_v = dot(put, vs, ((0,), (0,)))[0:CTOK_DEV]
+        new_cache[:, j * HD:(j + 1) * HD] = new_k.astype(bf16)
+        new_cache[:, (KVH + j) * HD:(KVH + j + 1) * HD] = new_v.astype(bf16)
+
+    @pl.loop(0, dsteps)
+    def _(c):
+        @pl.loop(1, N)
+        def _(k):
+            frm = lax.rem(me + k, N)
+            remote(
+                sbuf.at[0, 0], rbuf.at[c, frm], f_s.at[0, 0], f_r.at[c, frm], frm
+            ).wait_recv()
+
+        out[c] = (hst[c] + jnp.sum(rbuf[c].astype(f32), axis=0)).astype(bf16)
+
+    @pl.loop(1, N)
+    def _(k):
+        to = lax.rem(me + k, N)
+
+        @pl.when(to < HOLD)
+        def _():
+            remote(pack.at[to], packr.at[me], p_s.at[to], p_r.at[me], to).wait_send()
+
+        @pl.loop(0, dsteps)
+        def _(c):
+            give(c, to).wait_send()
+
+    @pl.when(holds)
+    def _():
+        @pl.loop(1, HOLD)
+        def _(k):
+            to = lax.rem(me + k, HOLD)
+            remote(kv.at[to], kvr.at[me], kv_s.at[to], kv_r.at[me], to).wait_send()
+
+        @pl.loop(1, N)
+        def _(k):
+            to = lax.rem(me + k, N)
+            remote(attn.at[to], attnr.at[me], a_s.at[to], a_r.at[me], to).wait_send()
+            remote(sent.at[to], got.at[me], t_s.at[to], t_r.at[me], to).wait_send()
+
+    @pl.loop(0, 15)
+    def _(i):
+        push(me, i, x_peer).wait_send()
+
+
+def fused(
+    old_cache, new_slot, lengths, old_angle, new_angle, queries, new_kv, resid, gain,
+    w_gate, w_up, w_down,
+):
+    bf16, f32 = jnp.bfloat16, jnp.float32
+    width = w_gate.shape[1]
+    model = w_gate.shape[0]
+
+    def by_head(a):
+        return a.reshape(2, KVH, GROUP, HD).transpose(1, 0, 2, 3).reshape(KVH, ROWS, HD)
+
+    own = new_kv.reshape(2, 2, KVH, HD).transpose(1, 2, 0, 3)
+    own = jnp.pad(own, ((0, 0), (0, 0), (0, ROWS - 2), (0, 0)))
+    pack = jnp.concatenate([by_head(queries), own[0], own[1]], axis=1)
+    vmem = pl.BlockSpec(memory_space=pltpu.VMEM)
+    smem = pl.BlockSpec(memory_space=pltpu.SMEM)
+    hbm = pl.BlockSpec(memory_space=pl.ANY)
+    dma = pltpu.SemaphoreType.DMA
+    dsteps = model // DC
+    new_cache, out = pl.pallas_call(
+        kernel,
+        out_shape=(
+            jax.ShapeDtypeStruct((CTOK_DEV, old_cache.shape[1]), bf16),
+            jax.ShapeDtypeStruct((KVH, ROWS, HD), bf16),
+        ),
+        in_specs=[vmem, vmem, smem, vmem, vmem, vmem, vmem, vmem, hbm, hbm, hbm],
+        out_specs=(vmem, vmem),
+        scratch_shapes=[
+            pltpu.VMEM((NG, KC, width), bf16),
+            pltpu.VMEM((NG, KC, width), bf16),
+            pltpu.VMEM((ND, width, DC), bf16),
+            pltpu.VMEM((KVH, 2, 128, HD), bf16),
+            pltpu.VMEM((HOLD, 2, 128, HD), bf16),
+            pltpu.VMEM((N, 48, HD), bf16),
+            pltpu.VMEM((N, ROWS, (KVH + 1) * HD), bf16),
+            pltpu.VMEM((HOLD, ROWS, (KVH + 1) * HD), bf16),
+            pltpu.VMEM((N, ROWS, HD), f32),
+            pltpu.VMEM((KVH, ROWS, HD), f32),
+            pltpu.VMEM((N, KVH, ROWS, HD), bf16),
+            pltpu.VMEM((256, HD), f32),
+            pltpu.VMEM((model // KC, 32, KC), bf16),
+            pltpu.VMEM((32, width), f32),
+            pltpu.VMEM((32, width), f32),
+            pltpu.VMEM((32, width), bf16),
+            pltpu.VMEM((256, HD), f32),
+            pltpu.VMEM((dsteps, N, ROWS, HD), bf16),
+            pltpu.VMEM((dsteps, N, ROWS, HD), bf16),
+            pltpu.VMEM((KVH, ROWS, HD), f32),
+            dma((NG,)), dma((NG,)), dma((ND,)),
+            dma((HOLD,)), dma((HOLD,)),
+            dma((N,)), dma((N,)),
+            dma((N,)), dma((HOLD,)),
+            dma((15,)), dma((N,)),
+            dma((N,)), dma((HOLD,)),
+            dma((dsteps, N)), dma((dsteps, N)),
+        ],
+        compiler_params=pltpu.CompilerParams(
+            collective_id=0, has_side_effects=True, vmem_limit_bytes=60 * 1024 * 1024
+        ),
+    )(
+        old_cache, new_slot.reshape(1, -1), lengths, old_angle, new_angle, pack,
+        by_head(resid), gain.reshape(KVH, GROUP, HD), w_gate, w_up, w_down,
+    )
+    out = out.reshape(KVH, 2, GROUP, HD).transpose(1, 0, 2, 3).reshape(2, model)
+    return new_cache, out
 
 
 def rotate_block(block, where_pos, old_angle, new_angle):
@@ -158,7 +581,7 @@
 
 def solution(mesh):
     return jax.shard_map(
-        per_device,
+        fused if mesh.shape["ctx"] == N else per_device,
         mesh=mesh,
         in_specs=(
             P(("groups", "ctx"), None),

time: 277 us -> 77.1 us (0.28)
  waiting for transfers between devices: 122 us -> 0 us
  Pallas kernels: 0 us -> 65.8 us
  blocking collectives: 47.7 us -> 0 us
  matrix products: 37.2 us -> 0 us
  starting transfers between devices: 22.1 us -> 0 us
  between operations: 15.1 us -> 0.64 us
  local copies, waits for them, and re-layouts: 21.3 us -> 9.61 us
  other arithmetic: 11 us -> 0.65 us
    unnamed x2 -> x0, waiting for transfers between devices: 88.4 us -> none
    pallas_call x0 -> x1, Pallas kernels: none -> 65.8 us  [fused(): pl.pallas_call(kernel, out_shape=(jax.ShapeDtypeStruct((CTOK_DEV, old_cac...]
    all_gather x2 -> x0, blocking collectives: 47.7 us -> none  [the longest x1 24.3 us: per_device(): piece = lax.all_gather(normed, 'ctx', axis=0, tiled=True)]
    dot_general x6 -> x0, matrix products: 37.2 us -> none  [the longest x1 22.6 us: per_device(): jnp.dot(hidden_all, w_down, preferred_element_type=jnp.float32)]
    all_to_all x5 -> x0, waiting for transfers between devices: 33.4 us -> none  [the longest x1 14.5 us: per_device(): lax.all_to_all(summed.reshape(devices, rows_dev, QH * HD), 'ctx', split_a...]
    all_to_all x5 -> x0, starting transfers between devices: 22.1 us -> none  [the longest x1 7.35 us: per_device(): lax.all_to_all(slot_info.reshape(devices, per_peer, 3), 'ctx', split_axis...]
    gather x4 -> x0, local copies, waits for them, and re-layouts: 3.56 us -> none  [the longest x1 1.72 us: per_device(): sent_rows = old_cache[sorted_order].reshape(devices, per_peer, row_width)]
    scatter x3 -> x0, local copies, waits for them, and re-layouts: 3.34 us -> none  [the longest x2 1.95 us: per_device(): jnp.zeros((CTOK_DEV,), jnp.int32).at[landing]]
  transfers between devices with their start and end apart: 6 -> 0, of which waited for: 5 -> 0; matrix products, arithmetic and copies ran while one was open for 8% -> 0% of each run, Pallas kernels for 0% -> 0%
where the time goes in v2:
time: 77.1 us; the launch traced here: 76.7 us
  Pallas kernels  65.8 us (85%)
  local copies, waits for them, and re-layouts  9.61 us (12%)
    pallas_call x1, Pallas kernels, fused(): pl.pallas_call(kernel, out_shape=(jax.ShapeDtypeStruct((CTOK_DEV, old_cac...  65.8 us
    unnamed x5, local copies, waits for them, and re-layouts  6.75 us
    reshape x2, local copies, waits for them, and re-layouts, by_head(): a.reshape(2, KVH, GROUP, HD).transpose(1, 0, 2, 3).reshape(KVH, ROWS, HD)  2.14 us

profile of v2, /device:TPU:0, one launch (start us, length us, event | category | flops | bytes accessed | tf_op | source)
XLA Modules:
  0.0 76.7 jit_solution(4404647025161291467)
XLA Ops:
  0.6 0.8 copy_bitcast_fusion.5
  1.4 1.4 %copy_bitcast_fusion.4.resid = bf16[8,16,128]{2,1,0:T(8,128)(2,1)} fusion(bf16[1,2,64,128]{3,1,2,0:T(2,128)(2,1)} %bitcast.39), kind=kLoop, calls=%fused_computation.9 | loop fusion | bytes 65536 | tf_op jit(solution)/shard_map/reshape | solution.py:378
  2.8 0.7 fusion
  3.5 0.6 pad_maximum_fusion.pack
  4.1 1.8 %copy.16.old_angle = f32[768,64]{1,0:T(8,128)} copy(f32[768,64]{0,1:T(8,128)} %param.15) | data formatting | bytes 393216 | tf_op args[3]
  6.0 1.8 %copy.17.new_angle = f32[768,64]{1,0:T(8,128)} copy(f32[768,64]{0,1:T(8,128)} %param.16) | data formatting | bytes 393216 | tf_op args[4]
  7.8 65.8 %shard_map.131 = (bf16[64,2048]{1,0:T(8,128)(2,1)}, bf16[8,16,128]{2,1,0:T(8,128)(2,1)}) custom-call(bf16[128,2048]{1,0:T(8,128)(2,1)} %old_cache.1, s32[1,128]{1,0:T(1,128)} %bitcast.43, s32[4]{0:T(128)} %lengths.1, f32[768,64]{1,0:T(8,128)} %copy.16.old_angle, f32[768,64]{1,0:T(8,128)} %copy.17.new_angle, bf16[8,48,128]{2,1,0:T(8,128)(2,1)} %pad_maximum_fusion.pack, ...), custom_call_target="tpu_custom_call" | custom-call | tf_op jit(solution)/shard_map/pallas_call | solution.py:388
  73.6 0.8 copy_bitcast_fusion.3
  74.3 0.6 copy.30
  75.0 1.7 %copy.32 = bf16[64,2048]{1,0:T(8,128)(2,1)} copy(bf16[64,2048]{1,0:T(8,128)(2,1)} %get-tuple-element.10) | data formatting | bytes 524288

commit v3 on v2

--- a/solution.py
+++ b/solution.py
@@ -17,7 +17,7 @@
 GROUP = QH // KVH
 ROWS = 16
 KC = 512
-NG = 10
+NG = 11
 DC = 1024
 ND = 3
 MESH = pl.DeviceIdType.MESH
@@ -45,9 +45,10 @@
 
 
 def kernel(
-    old_cache, slots, lengths, old_angle, new_angle, pack, resid, gain,
+    old_cache, slots, lengths, old_angle, new_angle, queries, own_kv, resid, gain,
     w_gate, w_up, w_down,
     new_cache, out,
+    packf, pack, tall,
     wg, wu, wd, kv, kvr, packr, sent, got, attn, attnr, norm, wide, xs, accg, accu,
     hidden, obuf, sbuf, rbuf, hst,
     g_sem, u_sem, d_sem, kv_s, kv_r, p_s, p_r, a_s, a_r, n_s, n_r, t_s, t_r, f_s, f_r,
@@ -87,6 +88,15 @@
     def _(c):
         fetch_out(c, c).start()
 
+    packf[...] = jnp.zeros_like(packf)
+    for j in range(KVH):
+        for g in range(GROUP):
+            cols = slice((j * GROUP + g) * HD, (j * GROUP + g + 1) * HD)
+            packf[j, pl.ds(g, 2, stride=GROUP), :] = queries[:, cols].astype(f32)
+        packf[j, 16:18, :] = own_kv[:, j * HD:(j + 1) * HD].astype(f32)
+        packf[j, 32:34, :] = own_kv[:, (KVH + j) * HD:(KVH + j + 1) * HD].astype(f32)
+    pack[...] = packf[...].astype(bf16)
+
     ends = [lengths[0]]
     for i in range(1, 4):
         ends.append(ends[-1] + lengths[i])
@@ -97,7 +107,7 @@
         prior = jnp.zeros((128, 1), jnp.int32)
         for i in range(4):
             prior = prior + jnp.where(tok >= ends[i], lengths[i], 0)
-        places = old_angle.shape[0]
+        places = old_angle.shape[1]
         pos = jnp.clip(tok - prior, 0, places - 1)
         pick = (lax.broadcasted_iota(jnp.int32, (128, places), 1) == pos).astype(f32).astype(bf16)
         d = new_angle[...] - old_angle[...]
@@ -105,7 +115,8 @@
         rest = d - d1.astype(f32)
         d2 = rest.astype(bf16)
         d3 = (rest - d2.astype(f32)).astype(bf16)
-        delta = dot(pick, d1) + dot(pick, d2) + dot(pick, d3)
+        last = ((1,), (1,))
+        delta = dot(pick, d1, last) + dot(pick, d2, last) + dot(pick, d3, last)
         delta = jnp.concatenate([delta, delta], axis=1)
         lane = lax.broadcasted_iota(jnp.int32, (128, 128), 1)
         cosine = jnp.cos(delta)
@@ -124,7 +135,7 @@
 
         @pl.when(to < HOLD)
         def _():
-            remote(pack.at[to], packr.at[me], p_s.at[to], p_r.at[me], to).start()
+            remote(pack.at[to], packr.at[me], p_s.at[to], p_r.at[0], to).start()
 
     @pl.when(holds)
     def _():
@@ -158,10 +169,8 @@
             vs = dot(perm, kv[j, 1]).reshape(N, PEER, HD)
             sent[:, :, j * HD:(j + 1) * HD] = jnp.concatenate([ks, vs], axis=1).astype(bf16)
 
-        @pl.loop(1, N)
-        def _(k):
-            frm = lax.rem(me + k, N)
-            remote(pack.at[0], packr.at[frm], p_s.at[0], p_r.at[frm], frm).wait_recv()
+        rest15 = packr.at[pl.ds(0, N - 1)]
+        remote(rest15, rest15, p_s.at[0], p_r.at[0], lax.rem(me + 1, N)).wait_recv()
 
         @pl.loop(1, HOLD)
         def _(k):
@@ -199,7 +208,15 @@
         @pl.loop(1, N)
         def _(k):
             to = lax.rem(me + k, N)
-            remote(attn.at[to], attnr.at[me], a_s.at[to], a_r.at[me], to).start()
+            remote(attn.at[to], attnr.at[me], a_s.at[0], a_r.at[me], to).start()
+
+    for j in range(KVH):
+        for g in range(GROUP):
+            cols = slice((j * GROUP + g) * HD, (j * GROUP + g + 1) * HD)
+            tall[0, j, pl.ds(g, 2, stride=GROUP), :] = resid[:, cols].astype(f32)
+            tall[1, j, pl.ds(g, 2, stride=GROUP), :] = jnp.broadcast_to(
+                gain[:, cols].astype(f32), (2, HD)
+            )
 
     @pl.loop(0, HOLD)
     def _(frm):
@@ -208,13 +225,13 @@
             other = lax.rem(me + 1, N)
             remote(attn.at[0], attnr.at[frm], a_s.at[0], a_r.at[frm], other).wait_recv()
 
-    h = resid[...].astype(f32) + attnr[...]
+    h = tall[0] + attnr[...]
     hst[...] = h
     h4 = h.reshape(KVH, 2, GROUP, HD)
     sq = jnp.sum(jnp.sum(h4 * h4, axis=0), axis=-1, keepdims=True)
     mean = jnp.sum(sq, axis=1, keepdims=True) / float(KVH * GROUP * HD)
     inv = lax.rsqrt(mean + 1e-05)
-    normed = h4 * inv[None] * gain[...].astype(f32).reshape(KVH, 1, GROUP, HD)
+    normed = h4 * inv[None] * tall[1].reshape(KVH, 2, GROUP, HD)
     norm[me] = normed.reshape(KVH, ROWS, HD).astype(bf16)
 
     z, x, core = me // 4, lax.rem(me // 2, 2), lax.rem(me, 2)
@@ -250,7 +267,7 @@
         @pl.loop(1, N)
         def _(k):
             to = lax.rem(me + k, N)
-            remote(sent.at[to], got.at[me], t_s.at[to], t_r.at[me], to).start()
+            remote(sent.at[to], got.at[me], t_s.at[0], t_r.at[me], to).start()
 
         got[me] = sent[me]
 
@@ -281,9 +298,14 @@
     gate = accg[...]
     hidden[...] = (gate / (1.0 + jnp.exp(-gate)) * accu[...]).astype(bf16)
 
-    def give(c, to):
+    def give(p, to):
+        two = pl.ds(2 * p, 2)
+        return remote(sbuf.at[two, to], rbuf.at[two, me], f_s.at[p], f_r.at[p], to)
+
+    def given(p):
+        two, some = pl.ds(2 * p, 2), pl.ds(0, N - 1)
         return remote(
-            sbuf.at[c, to], rbuf.at[c, me], f_s.at[c, to], f_r.at[c, me], to
+            sbuf.at[two, some], rbuf.at[two, some], f_s.at[p], f_r.at[p], lax.rem(me + 1, N)
         )
 
     @pl.loop(0, dsteps)
@@ -301,9 +323,11 @@
 
         rbuf[c, me] = sbuf[c, me]
 
-        @pl.loop(1, N)
-        def _(k):
-            give(c, lax.rem(me + k, N)).start()
+        @pl.when(lax.rem(c, 2) == 1)
+        def _():
+            @pl.loop(1, N)
+            def _(k):
+                give(c // 2, lax.rem(me + k, N)).start()
 
     @pl.loop(0, HOLD)
     def _(frm):
@@ -325,16 +349,13 @@
         new_cache[:, j * HD:(j + 1) * HD] = new_k.astype(bf16)
         new_cache[:, (KVH + j) * HD:(KVH + j + 1) * HD] = new_v.astype(bf16)
 
-    @pl.loop(0, dsteps)
-    def _(c):
-        @pl.loop(1, N)
-        def _(k):
-            frm = lax.rem(me + k, N)
-            remote(
-                sbuf.at[0, 0], rbuf.at[c, frm], f_s.at[0, 0], f_r.at[c, frm], frm
-            ).wait_recv()
-
-        out[c] = (hst[c] + jnp.sum(rbuf[c].astype(f32), axis=0)).astype(bf16)
+    for p in range(dsteps // 2):
+        given(p).wait_recv()
+        for c in (2 * p, 2 * p + 1):
+            hst[c] = hst[c] + jnp.sum(rbuf[c].astype(f32), axis=0)
+            for g in range(GROUP):
+                cols = slice((c * GROUP + g) * HD, (c * GROUP + g + 1) * HD)
+                out[:, cols] = hst[c, pl.ds(g, 2, stride=GROUP), :].astype(bf16)
 
     @pl.loop(1, N)
     def _(k):
@@ -342,11 +363,10 @@
 
         @pl.when(to < HOLD)
         def _():
-            remote(pack.at[to], packr.at[me], p_s.at[to], p_r.at[me], to).wait_send()
-
-        @pl.loop(0, dsteps)
-        def _(c):
-            give(c, to).wait_send()
+            remote(pack.at[to], packr.at[me], p_s.at[to], p_r.at[0], to).wait_send()
+
+    for p in range(dsteps // 2):
+        given(p).wait_send()
 
     @pl.when(holds)
     def _():
@@ -355,11 +375,10 @@
             to = lax.rem(me + k, HOLD)
             remote(kv.at[to], kvr.at[me], kv_s.at[to], kv_r.at[me], to).wait_send()
 
-        @pl.loop(1, N)
-        def _(k):
-            to = lax.rem(me + k, N)
-            remote(attn.at[to], attnr.at[me], a_s.at[to], a_r.at[me], to).wait_send()
-            remote(sent.at[to], got.at[me], t_s.at[to], t_r.at[me], to).wait_send()
+        other = lax.rem(me + 1, N)
+        out_a, out_t = attn.at[pl.ds(0, N - 1)], sent.at[pl.ds(0, N - 1)]
+        remote(out_a, out_a, a_s.at[0], a_r.at[me], other).wait_send()
+        remote(out_t, out_t, t_s.at[0], t_r.at[me], other).wait_send()
 
     @pl.loop(0, 15)
     def _(i):
@@ -374,12 +393,6 @@
     width = w_gate.shape[1]
     model = w_gate.shape[0]
 
-    def by_head(a):
-        return a.reshape(2, KVH, GROUP, HD).transpose(1, 0, 2, 3).reshape(KVH, ROWS, HD)
-
-    own = new_kv.reshape(2, 2, KVH, HD).transpose(1, 2, 0, 3)
-    own = jnp.pad(own, ((0, 0), (0, 0), (0, ROWS - 2), (0, 0)))
-    pack = jnp.concatenate([by_head(queries), own[0], own[1]], axis=1)
     vmem = pl.BlockSpec(memory_space=pltpu.VMEM)
     smem = pl.BlockSpec(memory_space=pltpu.SMEM)
     hbm = pl.BlockSpec(memory_space=pl.ANY)
@@ -389,11 +402,14 @@
         kernel,
         out_shape=(
             jax.ShapeDtypeStruct((CTOK_DEV, old_cache.shape[1]), bf16),
-            jax.ShapeDtypeStruct((KVH, ROWS, HD), bf16),
+            jax.ShapeDtypeStruct((2, model), bf16),
         ),
-        in_specs=[vmem, vmem, smem, vmem, vmem, vmem, vmem, vmem, hbm, hbm, hbm],
+        in_specs=[vmem, vmem, smem, vmem, vmem, vmem, vmem, vmem, vmem, hbm, hbm, hbm],
         out_specs=(vmem, vmem),
         scratch_shapes=[
+            pltpu.VMEM((KVH, 48, HD), f32),
+            pltpu.VMEM((KVH, 48, HD), bf16),
+            pltpu.VMEM((2, KVH, ROWS, HD), f32),
             pltpu.VMEM((NG, KC, width), bf16),
             pltpu.VMEM((NG, KC, width), bf16),
             pltpu.VMEM((ND, width, DC), bf16),
@@ -416,20 +432,19 @@
             pltpu.VMEM((KVH, ROWS, HD), f32),
             dma((NG,)), dma((NG,)), dma((ND,)),
             dma((HOLD,)), dma((HOLD,)),
-            dma((N,)), dma((N,)),
-            dma((N,)), dma((HOLD,)),
+            dma((N,)), dma((1,)),
+            dma((1,)), dma((HOLD,)),
             dma((15,)), dma((N,)),
-            dma((N,)), dma((HOLD,)),
-            dma((dsteps, N)), dma((dsteps, N)),
+            dma((1,)), dma((HOLD,)),
+            dma((dsteps // 2,)), dma((dsteps // 2,)),
         ],
         compiler_params=pltpu.CompilerParams(
             collective_id=0, has_side_effects=True, vmem_limit_bytes=60 * 1024 * 1024
         ),
     )(
-        old_cache, new_slot.reshape(1, -1), lengths, old_angle, new_angle, pack,
-        by_head(resid), gain.reshape(KVH, GROUP, HD), w_gate, w_up, w_down,
-    )
-    out = out.reshape(KVH, 2, GROUP, HD).transpose(1, 0, 2, 3).reshape(2, model)
+        old_cache, new_slot.reshape(1, -1), lengths, old_angle.T, new_angle.T, queries,
+        new_kv, resid, gain.reshape(1, -1), w_gate, w_up, w_down,
+    )
     return new_cache, out
 
 

time: 77.1 us -> 67.4 us (0.87)
  local copies, waits for them, and re-layouts: 9.61 us -> 4.42 us
  Pallas kernels: 65.8 us -> 62 us
    pallas_call x1, Pallas kernels: 65.8 us -> 62 us  [fused(): pl.pallas_call(kernel, out_shape=(jax.ShapeDtypeStruct((CTOK_DEV, old_cac...]
    unnamed x5 -> x2, local copies, waits for them, and re-layouts: 6.75 us -> 3.07 us
    reshape x2 -> x1, local copies, waits for them, and re-layouts: 2.14 us -> 1.35 us  [fused(): gain.reshape(1, -1)]
where the time goes in v3:
time: 67.4 us; the launch traced here: 67 us
  Pallas kernels  62 us (92%)
  local copies, waits for them, and re-layouts  4.42 us (7%)
    pallas_call x1, Pallas kernels, fused(): pl.pallas_call(kernel, out_shape=(jax.ShapeDtypeStruct((CTOK_DEV, old_cac...  62 us
    unnamed x2, local copies, waits for them, and re-layouts  3.07 us
    reshape x1, local copies, waits for them, and re-layouts, fused(): gain.reshape(1, -1)  1.35 us

profile of v3, /device:TPU:0, one launch (start us, length us, event | category | flops | bytes accessed | tf_op | source)
XLA Modules:
  0.0 67.0 jit_solution(657827154776090249)
XLA Ops:
  0.6 1.4 %reshape.11.gain = bf16[1,8192]{1,0:T(2,128)(2,1)} reshape(bf16[8192]{0:T(1024)(128)(2,1)} %param.20) | data formatting | bytes 32768 | tf_op jit(solution)/shard_map/reshape | solution.py:446
  2.0 62.0 %shard_map.131 = (bf16[64,2048]{1,0:T(8,128)(2,1)}, bf16[2,8192]{1,0:T(2,128)(2,1)}) custom-call(bf16[128,2048]{1,0:T(8,128)(2,1)} %old_cache.1, s32[1,128]{1,0:T(1,128)} %bitcast.5, s32[4]{0:T(128)} %lengths.1, f32[64,768]{1,0:T(8,128)} %bitcast.3, f32[64,768]{1,0:T(8,128)} %bitcast.4, bf16[2,8192]{1,0:T(2,128)(2,1)} %queries.1, bf16[2,2048]{1,0:T(2,128)(2,1)} %own_kv.1, ...), custom_call_target="tpu_custom_call" | custom-call | tf_op jit(solution)/shard_map/pallas_call | solution.py:401
  64.0 1.7 %copy.16 = bf16[64,2048]{1,0:T(8,128)(2,1)} copy(bf16[64,2048]{1,0:T(8,128)(2,1)} %get-tuple-element.4) | data formatting | bytes 524288
  65.7 1.4 %copy.17 = bf16[2,8192]{1,0:T(2,128)(2,1)} copy(bf16[2,8192]{1,0:T(2,128)(2,1)} %get-tuple-element.5) | data formatting | bytes 65536
